TPU v7x, 256 devices: a whole 4x4x8 slice. The times are simulated.
256 devices in a mesh: azi: 8 (over y, core), rad: 16 (over x, z_lo), axl: 2 (over z_hi).
Axes of the slice: x: 4, y: 4, z: 8 (z_hi: 2, z_lo: 4; z = z_hi * 4 + z_lo), core: 2. Of those that a mesh axis runs over, the one named last changes fastest.
Arguments:
- perturbation: float32 [5, 8, 1024, 2048], P(None, 'axl', 'rad', 'azi'), may hold values from -6 to 6
- axial_velocity: float32 [8, 1024], P('axl', 'rad'), may hold values from 0.4 to 1.2
- swirl_velocity: float32 [8, 1024], P('axl', 'rad'), may hold values from -0.8 to 0.8
- sound_speed: float32 [8, 1024], P('axl', 'rad'), may hold values from 1 to 1.6
- rotor_offset: int32 [1], replicated, may hold values from 0 to 2047
Outputs:
- tendency: float32 [5, 8, 1024, 2048], P(None, 'axl', 'rad', 'azi')
All inputs are finite; a program needn't handle non-finite values.
Results may differ from a plain program's by a relative error of at most 0.000065.
Values sent between devices are 32-bit elements; how exact they have to be, the bound alone decides.
No kernel may reach another device: no remote copies, remote signals or barrier semaphores. Data moves between devices by JAX's collectives and lax.ppermute only.
A program may use at most 128 MiB of HBM per device.

v0:
```python
import jax
import jax.numpy as jnp
import numpy as np
from jax import lax
from jax.sharding import PartitionSpec as P

NA = 2048
BAND = 128
WEIGHTS = (45.0 / 60.0, -9.0 / 60.0, 1.0 / 60.0)


def partner(value, axis, distance):
    mask = 2**distance
    pairs = [(source, source ^ mask) for source in range(lax.axis_size(axis))]
    return lax.ppermute(value, axis, pairs)


def with_halo(block, sides, width):
    for axis, dim in sides:
        count = lax.axis_size(axis)
        forward = [(i, i + 1) for i in range(count - 1)]
        backward = [(target, source) for source, target in forward]
        low = lax.ppermute(
            lax.slice_in_dim(block, block.shape[dim] - width, None, axis=dim), axis, forward
        )
        high = lax.ppermute(lax.slice_in_dim(block, 0, width, axis=dim), axis, backward)
        block = jnp.concatenate([low, block, high], axis=dim)
    return block


def stencil_coefs(cells, reach):
    offsets = np.arange(1, reach + 1)
    signs = np.where(offsets % 2 == 1, 1.0, -1.0)
    angles = np.pi * offsets / cells
    values = np.pi / cells * signs * np.cos(angles) / np.sin(angles)
    return np.concatenate([np.zeros(1), values])


def signed_table(coefs, offsets):
    reach = coefs.shape[0] - 1
    magnitude = np.abs(offsets)
    picked = coefs[np.minimum(magnitude, reach)]
    return np.where(magnitude <= reach, np.sign(offsets) * picked, 0.0)


def band_table(coefs, columns):
    reach = coefs.shape[0] - 1
    source = np.arange(columns + 2 * reach)
    target = np.arange(columns)
    offsets = source[:, None] - target[None, :] - reach
    return signed_table(coefs, offsets)


def central_diff(padded, axis_pos):
    extent = padded.shape[axis_pos] - 6
    result = jnp.zeros_like(lax.slice_in_dim(padded, 3, 3 + extent, axis=axis_pos))
    for reach_k, weight in enumerate(WEIGHTS, start=1):
        upper = lax.slice_in_dim(padded, 3 + reach_k, 3 + reach_k + extent, axis=axis_pos)
        lower = lax.slice_in_dim(padded, 3 - reach_k, 3 - reach_k + extent, axis=axis_pos)
        result = result + weight * (upper - lower)
    return result


def section_terms(padded, angular, axial_vel, swirl_vel, sound_vel, metric):
    deriv_x = central_diff(padded, 1)
    stream = axial_vel[:, :, None]
    turning = (swirl_vel * metric[None, :])[:, :, None]
    speed_sq = (sound_vel * sound_vel)[:, :, None]
    scale = metric[:, None]
    convect = stream * deriv_x + turning * angular
    spread = deriv_x[1] + scale * angular[3]
    return jnp.stack(
        [
            -(convect[0] + spread),
            -(convect[1] + deriv_x[4]),
            -convect[2],
            -(convect[3] + scale * angular[4]),
            -(convect[4] + speed_sq * spread),
        ]
    )


def radial_terms(radial, sound_vel):
    speed_sq = (sound_vel * sound_vel)[:, :, None]
    blank = jnp.zeros_like(radial[0])
    return jnp.stack([-radial[0], blank, -radial[1], blank, -speed_sq * radial[0]])


def make_metric(first_row, row_count, radial_total):
    index = (first_row + jnp.arange(row_count, dtype=jnp.int32)).astype(jnp.float32)
    return 2.0 / (1.0 + (index + 0.5) / radial_total)


def rotate_edge(edge_lines, start_cell):
    doubled = jnp.concatenate([edge_lines, edge_lines], axis=3)
    return lax.dynamic_slice_in_dim(doubled, start_cell, NA, 3)


def attach_planes(values, received, stator_side):
    blanks = jnp.zeros_like(received)
    lower = jnp.where(stator_side, blanks, received)
    upper = jnp.where(stator_side, received, blanks)
    return jnp.concatenate([lower, values, upper], axis=1)


def tiled_lines(lines_all, coefs):
    width = BAND
    blocks = NA // width
    lead = lines_all.shape[:3]
    tiles = lines_all.reshape(lead + (blocks, width))
    banded = band_table(coefs, width)
    left_part = jnp.asarray(banded[0:width], dtype=jnp.float32)
    middle_part = jnp.asarray(banded[width : 2 * width], dtype=jnp.float32)
    right_part = jnp.asarray(banded[2 * width : 3 * width], dtype=jnp.float32)
    form = "fxrke,ej->fxrkj"
    middle = jnp.einsum(
        form,
        tiles,
        middle_part,
        precision=lax.Precision.HIGHEST,
        preferred_element_type=jnp.float32,
    )
    from_left = jnp.einsum(
        form, tiles, left_part, precision=lax.Precision.HIGHEST, preferred_element_type=jnp.float32
    )
    from_right = jnp.einsum(
        form, tiles, right_part, precision=lax.Precision.HIGHEST, preferred_element_type=jnp.float32
    )
    result = middle + jnp.roll(from_left, 1, axis=3) + jnp.roll(from_right, -1, axis=3)
    return result.reshape(lines_all.shape)


def per_device(perturbation, axial_velocity, swirl_velocity, sound_speed, rotor_offset):
    azi_count = lax.axis_size("azi")
    rad_count = lax.axis_size("rad")
    rows = perturbation.shape[2]
    sub_rows = rows // azi_count
    azi_pos = lax.axis_index("azi")
    rad_pos = lax.axis_index("rad")
    axl_pos = lax.axis_index("axl")
    radial_total = rows * rad_count
    coefs = stencil_coefs(NA, BAND)
    shift_cells = rotor_offset[0]
    stator_side = axl_pos == 0
    start_cell = jnp.where(stator_side, shift_cells, NA - shift_cells) % NA
    lines_all = lax.all_to_all(perturbation, "azi", split_axis=2, concat_axis=3, tiled=True)
    angular = tiled_lines(lines_all, coefs)
    edge_lines = jnp.where(stator_side, lines_all[:, -3:], lines_all[:, :3])
    received = partner(rotate_edge(edge_lines, start_cell), "axl", 0)
    padded = attach_planes(lines_all, received, stator_side)
    row_start = azi_pos * sub_rows
    axial_sub = lax.dynamic_slice_in_dim(axial_velocity, row_start, sub_rows, 1)
    swirl_sub = lax.dynamic_slice_in_dim(swirl_velocity, row_start, sub_rows, 1)
    sound_sub = lax.dynamic_slice_in_dim(sound_speed, row_start, sub_rows, 1)
    metric = make_metric(rad_pos * rows + row_start, sub_rows, radial_total)
    partial_lines = section_terms(padded, angular, axial_sub, swirl_sub, sound_sub, metric)
    partial_value = lax.all_to_all(partial_lines, "azi", split_axis=3, concat_axis=2, tiled=True)
    pair = jnp.stack([perturbation[2], perturbation[4]])
    pair_pad = with_halo(pair, (("rad", 2),), 3)
    radial = central_diff(pair_pad, 2)
    return partial_value + radial_terms(radial, sound_speed)


def solution(mesh):
    return jax.shard_map(
        per_device,
        mesh=mesh,
        in_specs=(
            P(None, "axl", "rad", "azi"),
            P("axl", "rad"),
            P("axl", "rad"),
            P("axl", "rad"),
            P(),
        ),
        out_specs=P(None, "axl", "rad", "azi"),
        check_vma=False,
    )
```

profile of v0, /device:TPU:1, one launch (start us, length us, event | category | flops | bytes accessed | tf_op | source)
XLA Modules:
  0.0 211.9 jit_solution(11327305505855242520)
XLA Ops:
  0.0 3.5 %copy.17 = f32[5,4,64,256]{3,0,1,2:T(8,128)} copy(f32[5,4,64,256]{3,2,1,0:T(8,128)} %param.8) | data formatting | bytes 2621440 | tf_op args[0]
  3.5 6.7 %all-to-all-start = ((f32[5,4,64,256]{3,0,1,2:T(8,128)}), f32[5,4,64,256]{3,0,1,2:T(8,128)S(1)}, u32[]{:S(2)}, u32[]{:S(2)}) async-start(f32[5,4,64,256]{3,0,1,2:T(8,128)} %copy.17), calls=%async_computation | async-start | bytes 4194304 | tf_op jit(solution)/shard_map/all_to_all | solution.py:146
  10.2 1.1 fusion.32
  11.4 1.3 collective-permute-start.1
  12.7 4.0 %collective-permute-start.2 = (f32[2,4,3,256]{3,2,1,0:T(4,128)S(1)}, f32[2,4,3,256]{3,2,1,0:T(4,128)S(1)}, u32[]{:S(2)}, u32[]{:S(2)}) collective-permute-start(f32[2,4,3,256]{3,2,1,0:T(4,128)S(1)} %get-tuple-element.16), channel_id=1, source_target_pairs={{0,2},{2,4},{4,6},{6,8},{8,10},{10,12},{12,14},{14,16},{16,18},{18... | collective-permute-start | bytes 73736 | tf_op jit(solution)/shard_map/ppermute | solution.py:23
  16.7 0.1 dynamic-slice_multiply_fusion.1
  17.6 0.1 collective-permute-done.2
  17.7 0.9 pad_maximum_fusion.2
  18.6 18.0 %all-to-all-done = f32[5,4,64,256]{3,0,1,2:T(8,128)S(1)} async-done(((f32[5,4,64,256]{3,0,1,2:T(8,128)}), f32[5,4,64,256]{3,0,1,2:T(8,128)S(1)}, u32[]{:S(2)}, u32[]{:S(2)}) %all-to-all-start) | async-done | bytes 1310752 | tf_op jit(solution)/shard_map/all_to_all | solution.py:146
  36.6 1.3 copy-done.1
  37.9 2.4 %copy.25 = f32[5,4,8,8,256]{4,2,3,1,0:T(8,128)S(1)} copy(f32[5,4,8,8,256]{4,0,1,3,2:T(8,128)} %bitcast.54) | data formatting | bytes 2621440 | tf_op jit(solution)/shard_map/all_to_all | solution.py:146
  40.3 1.0 copy-done
  41.3 0.2 all_to_all.29
  41.5 1.4 reshape.55
  42.9 0.1 slice_select_fusion
  43.0 1.6 fusion.14
  44.5 6.1 %collective-permute-start = (f32[5,3,8,2048]{3,2,1,0:T(8,128)}, f32[5,3,8,2048]{3,2,1,0:T(8,128)}, u32[]{:S(2)}, u32[]{:S(2)}) collective-permute-start(f32[5,3,8,2048]{3,2,1,0:T(8,128)} %fusion.14), channel_id=1, source_target_pairs={{0,1},{1,0},{2,3},{3,2},{4,5},{5,4},{6,7},{7,6},{8,9},{9,8},{10,11... | collective-permute-start | bytes 2949128 | tf_op jit(solution)/shard_map/ppermute | solution.py:15
  50.7 1.2 convolution_bitcast_fusion
  51.9 0.1 slice.163
  52.1 0.6 copy-done.5
  52.7 1.2 convolution_bitcast_fusion.1
  54.0 2.5 %fusion.1 = f32[5,4,8,16,128]{4,3,2,1,0:T(8,128)} fusion(f32[128,128,1,1,1]{1,0,4,3,2:T(8,128)S(1)} %copy-done.4, f32[5,4,8,16,128]{4,3,2,1,0:T(8,128)S(1)} %reshape.55, f32[5,4,8,15,128]{4,3,2,1,0:T(8,128)S(1)} %bitcast.55, f32[5,4,8,1,128]{4,3,2,1,0:T(1,128)S(1)} %slice.161, f32[5,4,8,1,128]{4,3,2,1,0:T(1,128)S(1)} %slice.164, ...), kind=kOutput, calls=%fused_computation.14 | convolution fusion | flops 504627200 | bytes 5308416 | tf_op jit(solution)/shard_map/fxrke,ej->fxrkj/dot_general | solution.py:116
  56.5 1.5 reshape.56
  58.0 1.9 fusion.31
  59.9 1.0 squeeze.7
  60.9 1.7 squeeze.8
  62.6 14.3 %collective-permute-done = f32[5,3,8,2048]{3,2,1,0:T(8,128)} collective-permute-done((f32[5,3,8,2048]{3,2,1,0:T(8,128)}, f32[5,3,8,2048]{3,2,1,0:T(8,128)}, u32[]{:S(2)}, u32[]{:S(2)}) %collective-permute-start) | collective-permute-done | bytes 983072 | tf_op jit(solution)/shard_map/ppermute | solution.py:15
  76.9 1.4 broadcast_select_fusion.1
  78.3 1.1 multiply_add_fusion
  79.4 0.1 fusion.29
  79.6 0.7 copy-done.3
  80.4 0.1 fusion.24
  80.5 0.1 fusion.22
  80.6 12.5 %copy.19 = f32[5,4,8,2048]{2,1,0,3:T(4,128)} copy(f32[5,4,8,2048]{3,2,1,0:T(8,128)S(1)} %fusion.22) | data formatting | bytes 2621440 | tf_op jit(solution)/shard_map/stack | solution.py:72
  93.1 26.6 %reshape.60 = f32[8,1,40960]{2,1,0:T(1,128)} reshape(f32[2048,5,4,8]{3,2,1,0:T(4,128)} %bitcast.50) | data formatting | bytes 2621440
  119.8 20.2 %all-to-all-start.1 = ((f32[8,1,40960]{2,1,0:T(1,128)}), f32[8,1,40960]{2,1,0:T(1,128)S(1)}, u32[]{:S(2)}, u32[]{:S(2)}) async-start(f32[8,1,40960]{2,1,0:T(1,128)} %reshape.60), calls=%async_computation.1 | async-start | bytes 2621440 | tf_op jit(solution)/shard_map/all_to_all | solution.py:157
  140.0 0.3 fusion.16
  140.3 0.7 negate_dynamic-update-slice_fusion
  141.0 0.7 broadcast_dynamic-update-slice_fusion
  141.8 0.7 fusion.20
  142.5 0.7 broadcast_dynamic-update-slice_fusion.1
  143.2 0.8 multiply_dynamic-update-slice_fusion
  144.0 13.9 %all-to-all-done.1 = f32[8,1,40960]{2,1,0:T(1,128)S(1)} async-done(((f32[8,1,40960]{2,1,0:T(1,128)}), f32[8,1,40960]{2,1,0:T(1,128)S(1)}, u32[]{:S(2)}, u32[]{:S(2)}) %all-to-all-start.1) | async-done | bytes 1310752 | tf_op jit(solution)/shard_map/all_to_all | solution.py:157
  157.9 0.5 broadcast.89
  158.4 3.7 %reduce = f32[8,40960]{1,0:T(8,128)S(1)} reduce(f32[8,1,40960]{2,1,0:T(1,128)S(1)} %all-to-all-done.1, f32[]{:T(128)} %broadcast.89), dimensions={1}, to_apply=%all_to_all.30.reduce_sub_computation | reduce | bytes 2621444 | tf_op jit(solution)/shard_map/all_to_all | solution.py:157
  162.2 32.6 %reshape.61 = f32[2048,5,4,8]{3,2,1,0:T(4,128)} reshape(f32[8,40960]{1,0:T(8,128)S(1)} %reduce) | data formatting | bytes 2621440
  194.8 14.5 %copy.20 = f32[5,4,8,8,256]{4,3,2,1,0:T(8,128)S(1)} copy(f32[5,4,8,8,256]{3,1,0,4,2:T(4,128)} %bitcast.51) | data formatting | bytes 2621440 | tf_op jit(solution)/shard_map/all_to_all | solution.py:157
  209.4 2.6 %bitcast_add_fusion = f32[5,4,64,256]{3,2,1,0:T(8,128)} fusion(f32[5,4,64,256]{3,2,1,0:T(8,128)} %multiply_dynamic-update-slice_fusion, f32[5,4,8,8,256]{4,3,2,1,0:T(8,128)S(1)} %copy.20), kind=kLoop, calls=%fused_computation.29 | loop fusion | flops 327680 | bytes 3932160 | tf_op jit(solution)/shard_map/add | solution.py:161
  (25 shorter events, 0.3 us)
Async XLA Ops:
  3.5 33.1 %all-to-all-start = ((f32[5,4,64,256]{3,0,1,2:T(8,128)}), f32[5,4,64,256]{3,0,1,2:T(8,128)S(1)}, u32[]{:S(2)}, u32[]{:S(2)}) async-start(f32[5,4,64,256]{3,0,1,2:T(8,128)} %copy.17), calls=%async_computation | async-start | bytes 4194304 | tf_op jit(solution)/shard_map/all_to_all | solution.py:146
  10.2 6.5 %copy-start.7 = (f32[4,64]{1,0:T(4,128)S(1)}, f32[4,64]{1,0:T(4,128)}, u32[]{:S(2)}) copy-start(f32[4,64]{1,0:T(4,128)} %param.11) | copy-start | bytes 3076
  10.2 6.5 %copy-start.8 = (f32[4,64]{1,0:T(4,128)S(1)}, f32[4,64]{1,0:T(4,128)}, u32[]{:S(2)}) copy-start(f32[4,64]{1,0:T(4,128)} %param.10) | copy-start | bytes 3076
  10.2 6.5 %copy-start.9 = (f32[4,64]{1,0:T(4,128)S(1)}, f32[4,64]{1,0:T(4,128)}, u32[]{:S(2)}) copy-start(f32[4,64]{1,0:T(4,128)} %param.9) | copy-start | bytes 3076
  11.4 6.2 %collective-permute-start.1 = (f32[2,4,3,256]{3,2,1,0:T(4,128)S(1)}, f32[2,4,3,256]{3,2,1,0:T(4,128)S(1)}, u32[]{:S(2)}, u32[]{:S(2)}) collective-permute-start(f32[2,4,3,256]{3,2,1,0:T(4,128)S(1)} %get-tuple-element.15), channel_id=1, source_target_pairs={{2,0},{4,2},{6,4},{8,6},{10,8},{12,10},{14,12},{16,14},{18,16},{20... | collective-permute-start | bytes 73736 | tf_op jit(solution)/shard_map/ppermute | solution.py:26
  12.7 5.0 %collective-permute-start.2 = (f32[2,4,3,256]{3,2,1,0:T(4,128)S(1)}, f32[2,4,3,256]{3,2,1,0:T(4,128)S(1)}, u32[]{:S(2)}, u32[]{:S(2)}) collective-permute-start(f32[2,4,3,256]{3,2,1,0:T(4,128)S(1)} %get-tuple-element.16), channel_id=1, source_target_pairs={{0,2},{2,4},{4,6},{6,8},{8,10},{10,12},{12,14},{14,16},{16,18},{18... | collective-permute-start | bytes 73736 | tf_op jit(solution)/shard_map/ppermute | solution.py:23
  36.6 1.3 copy-start.1
  40.2 1.1 copy-start
  43.0 7.7 %copy-start.6 = (f32[128,128,1,1,1]{1,0,4,3,2:T(8,128)S(1)}, f32[128,128,1,1,1]{1,0,4,3,2:T(8,128)}, u32[]{:S(2)}) copy-start(f32[128,128,1,1,1]{1,0,4,3,2:T(8,128)} %constant.66) | copy-start | bytes 196612
  44.5 32.3 %collective-permute-start = (f32[5,3,8,2048]{3,2,1,0:T(8,128)}, f32[5,3,8,2048]{3,2,1,0:T(8,128)}, u32[]{:S(2)}, u32[]{:S(2)}) collective-permute-start(f32[5,3,8,2048]{3,2,1,0:T(8,128)} %fusion.14), channel_id=1, source_target_pairs={{0,1},{1,0},{2,3},{3,2},{4,5},{5,4},{6,7},{7,6},{8,9},{9,8},{10,11... | collective-permute-start | bytes 2949128 | tf_op jit(solution)/shard_map/ppermute | solution.py:15
  51.8 0.8 copy-start.5
  52.7 1.3 copy-start.4
  79.4 1.0 copy-start.3
  119.8 20.2 %copy-start.2 = (f32[2,4,67,256]{3,2,1,0:T(8,128)S(1)}, f32[2,4,67,256]{3,2,1,0:T(8,128)}, u32[]{:S(2)}) copy-start(f32[2,4,67,256]{3,2,1,0:T(8,128)} %get-tuple-element.14) | copy-start | bytes 1646596
  119.8 38.1 %all-to-all-start.1 = ((f32[8,1,40960]{2,1,0:T(1,128)}), f32[8,1,40960]{2,1,0:T(1,128)S(1)}, u32[]{:S(2)}, u32[]{:S(2)}) async-start(f32[8,1,40960]{2,1,0:T(1,128)} %reshape.60), calls=%async_computation.1 | async-start | bytes 2621440 | tf_op jit(solution)/shard_map/all_to_all | solution.py:157
where the time goes:
time: 213 us; the launch traced here: 212 us
  local copies, waits for them, and re-layouts  107 us (50%)
  waiting for transfers between devices  46.3 us (22%)
  starting transfers between devices  38.4 us (18%)
  other arithmetic  14.5 us (7%)
  matrix products  4.92 us (2%)
    unnamed x25, local copies, waits for them, and re-layouts  68 us
    all_to_all x1, starting transfers between devices, per_device(): lax.all_to_all(partial_lines, 'azi', split_axis=3, concat_axis=2, tiled=T...  20.2 us
    all_to_all x1, waiting for transfers between devices, per_device(): lax.all_to_all(perturbation, 'azi', split_axis=2, concat_axis=3, tiled=True)  18 us
    all_to_all x2, local copies, waits for them, and re-layouts, per_device(): lax.all_to_all(partial_lines, 'azi', split_axis=3, concat_axis=2, tiled=T...  15.1 us
    ppermute x1, waiting for transfers between devices, partner(): return lax.ppermute(value, axis, pairs)  14.3 us
    all_to_all x1, waiting for transfers between devices, per_device(): lax.all_to_all(partial_lines, 'azi', split_axis=3, concat_axis=2, tiled=T...  13.9 us
    another operation x1, local copies, waits for them, and re-layouts, section_terms(): jnp.stack([-(convect[0] + spread), -(convect[1] + deriv_x[4]), -convect[2...  12.5 us
    all_to_all x1, starting transfers between devices, per_device(): lax.all_to_all(perturbation, 'azi', split_axis=2, concat_axis=3, tiled=True)  6.74 us
  transfers between devices with their start and end apart: 5, of which 4 were waited for; matrix products, arithmetic and copies ran while one was open for 8% of the time, Pallas kernels for 0%

commit v1 on v0

--- a/solution.py
+++ b/solution.py
@@ -7,6 +7,28 @@
 NA = 2048
 BAND = 128
 WEIGHTS = (45.0 / 60.0, -9.0 / 60.0, 1.0 / 60.0)
+
+
+def in_blocks(x, dim, size):
+    before, after = (x.shape[:dim], x.shape[dim + 1 :])
+    return jnp.moveaxis(x.reshape(*before, size, -1, *after), dim, 0)
+
+
+def laid_out(parts, dim):
+    parts = jnp.moveaxis(parts, 0, dim)
+    lengths = parts.shape
+    return parts.reshape(*lengths[:dim], lengths[dim] * lengths[dim + 1], *lengths[dim + 2 :])
+
+
+def exchange_in_pairs(shard, axis, split_dim, concat_dim):
+    size, index = (lax.axis_size(axis), lax.axis_index(axis))
+    tiles = in_blocks(shard, split_dim, size)
+    done = [tiles[index]]
+    for step in range(1, size):
+        sent = tiles[index ^ step]
+        done.append(lax.ppermute(sent, axis, [(i, i ^ step) for i in range(size)]))
+    tiles = jnp.stack(done)[index ^ jnp.arange(size)]
+    return laid_out(tiles, concat_dim)
 
 
 def partner(value, axis, distance):
@@ -154,7 +176,7 @@
     sound_sub = lax.dynamic_slice_in_dim(sound_speed, row_start, sub_rows, 1)
     metric = make_metric(rad_pos * rows + row_start, sub_rows, radial_total)
     partial_lines = section_terms(padded, angular, axial_sub, swirl_sub, sound_sub, metric)
-    partial_value = lax.all_to_all(partial_lines, "azi", split_axis=3, concat_axis=2, tiled=True)
+    partial_value = exchange_in_pairs(partial_lines, "azi", 3, 2)
     pair = jnp.stack([perturbation[2], perturbation[4]])
     pair_pad = with_halo(pair, (("rad", 2),), 3)
     radial = central_diff(pair_pad, 2)

time: 213 us -> 128 us (0.60)
  local copies, waits for them, and re-layouts: 107 us -> 12.8 us
  waiting for transfers between devices: 46.3 us -> 53.5 us
  starting transfers between devices: 38.4 us -> 44.3 us
  other arithmetic: 14.5 us -> 9.85 us
    unnamed x25 -> x34, local copies, waits for them, and re-layouts: 68 us -> 5.57 us
    ppermute x0 -> x7, starting transfers between devices: none -> 25.5 us  [exchange_in_pairs(): done.append(lax.ppermute(sent, axis, [(i, i ^ step) for i in range(size)]))]
    all_to_all x1 -> x0, starting transfers between devices: 20.2 us -> none  [per_device(): lax.all_to_all(partial_lines, 'azi', split_axis=3, concat_axis=2, tiled=T...]
    all_to_all x2 -> x0, local copies, waits for them, and re-layouts: 15.1 us -> none  [per_device(): lax.all_to_all(partial_lines, 'azi', split_axis=3, concat_axis=2, tiled=T...]
    all_to_all x1 -> x0, waiting for transfers between devices: 13.9 us -> none  [per_device(): lax.all_to_all(partial_lines, 'azi', split_axis=3, concat_axis=2, tiled=T...]
    ppermute x0 -> x7, waiting for transfers between devices: none -> 13.9 us  [exchange_in_pairs(): done.append(lax.ppermute(sent, axis, [(i, i ^ step) for i in range(size)]))]
    another operation x1, local copies, waits for them, and re-layouts: 12.5 us -> 0.02 us  [section_terms(): jnp.stack([-(convect[0] + spread), -(convect[1] + deriv_x[4]), -convect[2...]
    all_to_all x1, waiting for transfers between devices: 18 us -> 22 us  [per_device(): lax.all_to_all(perturbation, 'azi', split_axis=2, concat_axis=3, tiled=True)]
  transfers between devices with their start and end apart: 5 -> 11, of which waited for: 4 -> 7; matrix products, arithmetic and copies ran while one was open for 8% -> 11% of each run, Pallas kernels for 0% -> 0%
where the time goes in v1:
time: 128 us; the launch traced here: 126 us
  waiting for transfers between devices  53.5 us (42%)
  starting transfers between devices  44.3 us (35%)
  local copies, waits for them, and re-layouts  12.8 us (10%)
  other arithmetic  9.85 us (8%)
  matrix products  4.95 us (4%)
    ppermute x7, starting transfers between devices, exchange_in_pairs(): done.append(lax.ppermute(sent, axis, [(i, i ^ step) for i in range(size)]))  25.5 us
    all_to_all x1, waiting for transfers between devices, per_device(): lax.all_to_all(perturbation, 'azi', split_axis=2, concat_axis=3, tiled=True)  22 us
    ppermute x1, waiting for transfers between devices, partner(): return lax.ppermute(value, axis, pairs)  17.6 us
    ppermute x7, waiting for transfers between devices, exchange_in_pairs(): done.append(lax.ppermute(sent, axis, [(i, i ^ step) for i in range(size)]))  13.9 us
    all_to_all x1, starting transfers between devices, per_device(): lax.all_to_all(perturbation, 'azi', split_axis=2, concat_axis=3, tiled=True)  6.42 us
    ppermute x1, starting transfers between devices, partner(): return lax.ppermute(value, axis, pairs)  6.12 us
    unnamed x34, local copies, waits for them, and re-layouts  5.57 us
    ppermute x1, starting transfers between devices, with_halo(): lax.ppermute(lax.slice_in_dim(block, block.shape[dim] - width, None, axis...  5 us
  transfers between devices with their start and end apart: 11, of which 7 were waited for; matrix products, arithmetic and copies ran while one was open for 11% of the time, Pallas kernels for 0%

profile of v1, /device:TPU:1, one launch (start us, length us, event | category | flops | bytes accessed | tf_op | source)
XLA Modules:
  0.0 126.5 jit_solution(8952857609758073742)
XLA Ops:
  0.0 1.2 fusion.30
  1.2 1.3 %collective-permute-start.8 = (f32[2,4,3,256]{3,2,1,0:T(4,128)S(1)}, f32[2,4,3,256]{3,2,1,0:T(4,128)S(1)}, u32[]{:S(2)}, u32[]{:S(2)}) collective-permute-start(f32[2,4,3,256]{3,2,1,0:T(4,128)S(1)} %get-tuple-element.27), channel_id=1, source_target_pairs={{2,0},{4,2},{6,4},{8,6},{10,8},{12,10},{14,12},{16,14},{18,16},{20... | collective-permute-start | bytes 73736 | tf_op jit(solution)/shard_map/ppermute | solution.py:48
  2.5 5.0 %collective-permute-start.9 = (f32[2,4,3,256]{3,2,1,0:T(4,128)S(1)}, f32[2,4,3,256]{3,2,1,0:T(4,128)S(1)}, u32[]{:S(2)}, u32[]{:S(2)}) collective-permute-start(f32[2,4,3,256]{3,2,1,0:T(4,128)S(1)} %get-tuple-element.28), channel_id=1, source_target_pairs={{0,2},{2,4},{4,6},{6,8},{8,10},{10,12},{12,14},{14,16},{16,18},{18... | collective-permute-start | bytes 73736 | tf_op jit(solution)/shard_map/ppermute | solution.py:45
  7.5 2.2 %copy.31 = f32[5,4,64,256]{3,0,1,2:T(8,128)} copy(f32[5,4,64,256]{3,2,1,0:T(8,128)S(1)} %copy-done.3) | data formatting | bytes 2621440 | tf_op args[0]
  9.7 6.4 %all-to-all-start = ((f32[5,4,64,256]{3,0,1,2:T(8,128)}), f32[5,4,64,256]{3,0,1,2:T(8,128)S(1)}, u32[]{:S(2)}, u32[]{:S(2)}) async-start(f32[5,4,64,256]{3,0,1,2:T(8,128)} %copy.31), calls=%async_computation | async-start | bytes 4194304 | tf_op jit(solution)/shard_map/all_to_all | solution.py:168
  16.2 0.1 constant_dynamic-slice_fusion.2
  17.1 0.1 pad_maximum_fusion.2
  17.2 0.3 fusion.16
  17.5 0.8 negate_dynamic-update-slice_fusion
  18.3 0.7 broadcast_dynamic-update-slice_fusion
  19.0 0.7 fusion.20
  19.7 0.7 broadcast_dynamic-update-slice_fusion.1
  20.5 22.0 %all-to-all-done = f32[5,4,64,256]{3,0,1,2:T(8,128)S(1)} async-done(((f32[5,4,64,256]{3,0,1,2:T(8,128)}), f32[5,4,64,256]{3,0,1,2:T(8,128)S(1)}, u32[]{:S(2)}, u32[]{:S(2)}) %all-to-all-start) | async-done | bytes 1310752 | tf_op jit(solution)/shard_map/all_to_all | solution.py:168
  42.5 0.8 copy.53
  43.2 1.1 copy-done
  44.3 0.1 reshape.95
  44.4 1.5 %all_to_all.16 = f32[5,4,8,2048]{3,2,1,0:T(8,128)S(1)} reshape(f32[5,4,8,8,256]{4,3,2,1,0:T(8,128)} %bitcast.102) | data formatting | bytes 2621440 | tf_op jit(solution)/shard_map/all_to_all | solution.py:168
  45.9 0.1 slice_select_fusion
  46.0 1.5 %fusion.14 = f32[5,3,8,2048]{3,2,1,0:T(8,128)} fusion(s32[]{:T(128)S(6)} %select_n.73, f32[5,3,8,2048]{3,2,1,0:T(8,128)S(1)} %slice_select_fusion), kind=kLoop, calls=%fused_computation.33 | loop fusion | flops 245760 | bytes 1966084 | tf_op jit(solution)/shard_map/concatenate | solution.py:117
  47.6 6.1 %collective-permute-start = (f32[5,3,8,2048]{3,2,1,0:T(8,128)}, f32[5,3,8,2048]{3,2,1,0:T(8,128)}, u32[]{:S(2)}, u32[]{:S(2)}) collective-permute-start(f32[5,3,8,2048]{3,2,1,0:T(8,128)} %fusion.14), channel_id=1, source_target_pairs={{0,1},{1,0},{2,3},{3,2},{4,5},{5,4},{6,7},{7,6},{8,9},{9,8},{10,11... | collective-permute-start | bytes 2949128 | tf_op jit(solution)/shard_map/ppermute | solution.py:37
  53.7 1.2 convolution_bitcast_fusion
  54.9 0.1 slice.165
  55.1 0.7 copy-done.5
  55.8 1.2 convolution_bitcast_fusion.1
  57.0 0.1 slice.163
  57.1 2.6 %fusion.1 = f32[5,4,8,16,128]{4,3,2,1,0:T(8,128)} fusion(f32[128,128,1,1,1]{1,0,4,3,2:T(8,128)S(1)} %copy-done.4, f32[5,4,8,16,128]{4,3,2,1,0:T(8,128)S(1)} %reshape.95, f32[5,4,8,15,128]{4,3,2,1,0:T(8,128)S(1)} %bitcast.104, f32[5,4,8,1,128]{4,3,2,1,0:T(1,128)S(1)} %slice.163, f32[5,4,8,1,128]{4,3,2,1,0:T(1,128)S(1)} %slice.166, ...), kind=kOutput, calls=%fused_computation.15 | convolution fusion | flops 504627200 | bytes 5308416 | tf_op jit(solution)/shard_map/fxrke,ej->fxrkj/dot_general | solution.py:138
  59.6 1.5 %reshape.96 = f32[5,4,8,2048]{3,2,1,0:T(8,128)S(1)} reshape(f32[5,4,8,16,128]{4,3,2,1,0:T(8,128)} %fusion.1) | data formatting | bytes 2621440 | tf_op jit(solution)/shard_map/reshape | solution.py:152
  61.1 1.1 fusion.29
  62.3 17.6 %collective-permute-done = f32[5,3,8,2048]{3,2,1,0:T(8,128)} collective-permute-done((f32[5,3,8,2048]{3,2,1,0:T(8,128)}, f32[5,3,8,2048]{3,2,1,0:T(8,128)}, u32[]{:S(2)}, u32[]{:S(2)}) %collective-permute-start) | collective-permute-done | bytes 983072 | tf_op jit(solution)/shard_map/ppermute | solution.py:37
  79.9 1.4 %broadcast_select_fusion.1 = (f32[5,3,8,2048]{3,2,1,0:T(8,128)S(1)}, f32[5,3,8,2048]{3,2,1,0:T(8,128)S(1)}) fusion(f32[5,3,8,2048]{3,2,1,0:T(8,128)} %collective-permute-done, pred[]{:T(512)S(6)} %eq.5), kind=kLoop, calls=%fused_computation.46 | loop fusion | flops 491520 | bytes 2949121 | tf_op jit(solution)/shard_map/jit(_where)/select_n | solution.py:124
  81.3 1.1 multiply_add_fusion
  82.4 0.2 fusion.21
  82.8 0.1 dynamic-slice_bitcast_fusion
  82.9 16.7 %collective-permute-start.1 = (f32[5,4,8,256]{3,2,1,0:T(8,128)S(1)}, f32[5,4,8,256]{3,2,1,0:T(8,128)S(1)}, u32[]{:S(2)}, u32[]{:S(2)}) collective-permute-start(f32[5,4,8,256]{3,2,1,0:T(8,128)S(1)} %get-tuple-element.17), channel_id=1, source_target_pairs={{0,32},{32,0},{64,96},{96,64},{128,160},{160,128},{192,224},{224,1... | collective-permute-start | bytes 491528 | tf_op jit(solution)/shard_map/ppermute | solution.py:29
  99.6 0.8 multiply_dynamic-update-slice_fusion
  100.4 0.3 collective-permute-start.2
  100.7 2.1 %collective-permute-start.3 = (f32[5,4,8,256]{3,2,1,0:T(8,128)S(1)}, f32[5,4,8,256]{3,2,1,0:T(8,128)S(1)}, u32[]{:S(2)}, u32[]{:S(2)}) collective-permute-start(f32[5,4,8,256]{3,2,1,0:T(8,128)S(1)} %get-tuple-element.15), channel_id=1, source_target_pairs={{0,96},{32,64},{64,32},{96,0},{128,224},{160,192},{192,160},{224,1... | collective-permute-start | bytes 491528 | tf_op jit(solution)/shard_map/ppermute | solution.py:29
  102.8 0.4 collective-permute-start.4
  103.2 2.2 %collective-permute-start.5 = (f32[5,4,8,256]{3,2,1,0:T(8,128)S(1)}, f32[5,4,8,256]{3,2,1,0:T(8,128)S(1)}, u32[]{:S(2)}, u32[]{:S(2)}) collective-permute-start(f32[5,4,8,256]{3,2,1,0:T(8,128)S(1)} %get-tuple-element.13), channel_id=1, source_target_pairs={{0,160},{32,128},{64,224},{96,192},{128,32},{160,0},{192,96},{224,... | collective-permute-start | bytes 491528 | tf_op jit(solution)/shard_map/ppermute | solution.py:29
  105.5 1.0 collective-permute-start.6
  106.5 2.8 %collective-permute-start.7 = (f32[5,4,8,256]{3,2,1,0:T(8,128)S(1)}, f32[5,4,8,256]{3,2,1,0:T(8,128)S(1)}, u32[]{:S(2)}, u32[]{:S(2)}) collective-permute-start(f32[5,4,8,256]{3,2,1,0:T(8,128)S(1)} %get-tuple-element.11), channel_id=1, source_target_pairs={{0,224},{32,192},{64,160},{96,128},{128,96},{160,64},{192,32},{224... | collective-permute-start | bytes 491528 | tf_op jit(solution)/shard_map/ppermute | solution.py:29
  109.3 2.1 %collective-permute-done.3 = f32[5,4,8,256]{3,2,1,0:T(8,128)S(1)} collective-permute-done((f32[5,4,8,256]{3,2,1,0:T(8,128)S(1)}, f32[5,4,8,256]{3,2,1,0:T(8,128)S(1)}, u32[]{:S(2)}, u32[]{:S(2)}) %collective-permute-start.3) | collective-permute-done | bytes 163872 | tf_op jit(solution)/shard_map/ppermute | solution.py:29
  111.4 1.6 %collective-permute-done.4 = f32[5,4,8,256]{3,2,1,0:T(8,128)S(1)} collective-permute-done((f32[5,4,8,256]{3,2,1,0:T(8,128)S(1)}, f32[5,4,8,256]{3,2,1,0:T(8,128)S(1)}, u32[]{:S(2)}, u32[]{:S(2)}) %collective-permute-start.4) | collective-permute-done | bytes 163872 | tf_op jit(solution)/shard_map/ppermute | solution.py:29
  113.1 4.5 %collective-permute-done.5 = f32[5,4,8,256]{3,2,1,0:T(8,128)S(1)} collective-permute-done((f32[5,4,8,256]{3,2,1,0:T(8,128)S(1)}, f32[5,4,8,256]{3,2,1,0:T(8,128)S(1)}, u32[]{:S(2)}, u32[]{:S(2)}) %collective-permute-start.5) | collective-permute-done | bytes 163872 | tf_op jit(solution)/shard_map/ppermute | solution.py:29
  117.6 1.7 %collective-permute-done.6 = f32[5,4,8,256]{3,2,1,0:T(8,128)S(1)} collective-permute-done((f32[5,4,8,256]{3,2,1,0:T(8,128)S(1)}, f32[5,4,8,256]{3,2,1,0:T(8,128)S(1)}, u32[]{:S(2)}, u32[]{:S(2)}) %collective-permute-start.6) | collective-permute-done | bytes 163872 | tf_op jit(solution)/shard_map/ppermute | solution.py:29
  119.3 3.9 %collective-permute-done.7 = f32[5,4,8,256]{3,2,1,0:T(8,128)S(1)} collective-permute-done((f32[5,4,8,256]{3,2,1,0:T(8,128)S(1)}, f32[5,4,8,256]{3,2,1,0:T(8,128)S(1)}, u32[]{:S(2)}, u32[]{:S(2)}) %collective-permute-start.7) | collective-permute-done | bytes 163872 | tf_op jit(solution)/shard_map/ppermute | solution.py:29
  123.2 0.6 gather_fusion
  123.9 2.6 %bitcast_add_fusion = f32[5,4,64,256]{3,2,1,0:T(8,128)} fusion(f32[5,4,64,256]{3,2,1,0:T(8,128)} %multiply_dynamic-update-slice_fusion, f32[8,5,4,8,256]{4,3,2,1,0:T(8,128)S(1)} %gather_fusion), kind=kLoop, calls=%fused_computation.30 | loop fusion | flops 327680 | bytes 3932160 | tf_op jit(solution)/shard_map/add | solution.py:183
  (44 shorter events, 0.5 us)
Async XLA Ops:
  0.0 7.5 %copy-start.3 = (f32[5,4,64,256]{3,2,1,0:T(8,128)S(1)}, f32[5,4,64,256]{3,2,1,0:T(8,128)}, u32[]{:S(2)}) copy-start(f32[5,4,64,256]{3,2,1,0:T(8,128)} %param.8) | copy-start | bytes 3932164
  1.2 15.9 %collective-permute-start.8 = (f32[2,4,3,256]{3,2,1,0:T(4,128)S(1)}, f32[2,4,3,256]{3,2,1,0:T(4,128)S(1)}, u32[]{:S(2)}, u32[]{:S(2)}) collective-permute-start(f32[2,4,3,256]{3,2,1,0:T(4,128)S(1)} %get-tuple-element.27), channel_id=1, source_target_pairs={{2,0},{4,2},{6,4},{8,6},{10,8},{12,10},{14,12},{16,14},{18,16},{20... | collective-permute-start | bytes 73736 | tf_op jit(solution)/shard_map/ppermute | solution.py:48
  2.5 14.6 %collective-permute-start.9 = (f32[2,4,3,256]{3,2,1,0:T(4,128)S(1)}, f32[2,4,3,256]{3,2,1,0:T(4,128)S(1)}, u32[]{:S(2)}, u32[]{:S(2)}) collective-permute-start(f32[2,4,3,256]{3,2,1,0:T(4,128)S(1)} %get-tuple-element.28), channel_id=1, source_target_pairs={{0,2},{2,4},{4,6},{6,8},{8,10},{10,12},{12,14},{14,16},{16,18},{18... | collective-permute-start | bytes 73736 | tf_op jit(solution)/shard_map/ppermute | solution.py:45
  9.7 6.4 %copy-start.7 = (f32[4,64]{1,0:T(4,128)S(1)}, f32[4,64]{1,0:T(4,128)}, u32[]{:S(2)}) copy-start(f32[4,64]{1,0:T(4,128)} %param.11) | copy-start | bytes 3076
  9.7 6.5 %copy-start.8 = (f32[4,64]{1,0:T(4,128)S(1)}, f32[4,64]{1,0:T(4,128)}, u32[]{:S(2)}) copy-start(f32[4,64]{1,0:T(4,128)} %param.9) | copy-start | bytes 3076
  9.7 6.5 %copy-start.9 = (f32[4,64]{1,0:T(4,128)S(1)}, f32[4,64]{1,0:T(4,128)}, u32[]{:S(2)}) copy-start(f32[4,64]{1,0:T(4,128)} %param.10) | copy-start | bytes 3076
  9.7 32.8 %all-to-all-start = ((f32[5,4,64,256]{3,0,1,2:T(8,128)}), f32[5,4,64,256]{3,0,1,2:T(8,128)S(1)}, u32[]{:S(2)}, u32[]{:S(2)}) async-start(f32[5,4,64,256]{3,0,1,2:T(8,128)} %copy.31), calls=%async_computation | async-start | bytes 4194304 | tf_op jit(solution)/shard_map/all_to_all | solution.py:168
  17.5 2.2 %copy-start.1 = (f32[2,4,64,256]{3,2,1,0:T(8,128)}, f32[2,4,64,256]{3,2,1,0:T(8,128)S(1)}, u32[]{:S(2)}) copy-start(f32[2,4,64,256]{3,2,1,0:T(8,128)S(1)} %fusion.16) | copy-start | bytes 1572868
  43.2 1.1 copy-start
  46.0 7.7 %copy-start.6 = (f32[128,128,1,1,1]{1,0,4,3,2:T(8,128)S(1)}, f32[128,128,1,1,1]{1,0,4,3,2:T(8,128)}, u32[]{:S(2)}) copy-start(f32[128,128,1,1,1]{1,0,4,3,2:T(8,128)} %constant.82) | copy-start | bytes 196612
  47.6 32.3 %collective-permute-start = (f32[5,3,8,2048]{3,2,1,0:T(8,128)}, f32[5,3,8,2048]{3,2,1,0:T(8,128)}, u32[]{:S(2)}, u32[]{:S(2)}) collective-permute-start(f32[5,3,8,2048]{3,2,1,0:T(8,128)} %fusion.14), channel_id=1, source_target_pairs={{0,1},{1,0},{2,3},{3,2},{4,5},{5,4},{6,7},{7,6},{8,9},{9,8},{10,11... | collective-permute-start | bytes 2949128 | tf_op jit(solution)/shard_map/ppermute | solution.py:37
  54.9 0.8 copy-start.5
  55.8 1.3 %copy-start.4 = (f32[128,128,1,1,1]{1,0,4,3,2:T(8,128)S(1)}, f32[128,128,1,1,1]{1,0,4,3,2:T(8,128)}, u32[]{:S(2)}) copy-start(f32[128,128,1,1,1]{1,0,4,3,2:T(8,128)} %constant.80) | copy-start | bytes 196612
  82.8 16.9 %copy-start.2 = (f32[2,4,64,256]{3,2,1,0:T(8,128)S(1)}, f32[2,4,64,256]{3,2,1,0:T(8,128)}, u32[]{:S(2)}) copy-start(f32[2,4,64,256]{3,2,1,0:T(8,128)} %copy-done.1) | copy-start | bytes 1572868
  82.9 22.5 %collective-permute-start.1 = (f32[5,4,8,256]{3,2,1,0:T(8,128)S(1)}, f32[5,4,8,256]{3,2,1,0:T(8,128)S(1)}, u32[]{:S(2)}, u32[]{:S(2)}) collective-permute-start(f32[5,4,8,256]{3,2,1,0:T(8,128)S(1)} %get-tuple-element.17), channel_id=1, source_target_pairs={{0,32},{32,0},{64,96},{96,64},{128,160},{160,128},{192,224},{224,1... | collective-permute-start | bytes 491528 | tf_op jit(solution)/shard_map/ppermute | solution.py:29
  100.4 6.0 %collective-permute-start.2 = (f32[5,4,8,256]{3,2,1,0:T(8,128)S(1)}, f32[5,4,8,256]{3,2,1,0:T(8,128)S(1)}, u32[]{:S(2)}, u32[]{:S(2)}) collective-permute-start(f32[5,4,8,256]{3,2,1,0:T(8,128)S(1)} %get-tuple-element.16), channel_id=1, source_target_pairs={{0,64},{32,96},{64,0},{96,32},{128,192},{160,224},{192,128},{224,1... | collective-permute-start | bytes 491528 | tf_op jit(solution)/shard_map/ppermute | solution.py:29
  100.7 10.7 %collective-permute-start.3 = (f32[5,4,8,256]{3,2,1,0:T(8,128)S(1)}, f32[5,4,8,256]{3,2,1,0:T(8,128)S(1)}, u32[]{:S(2)}, u32[]{:S(2)}) collective-permute-start(f32[5,4,8,256]{3,2,1,0:T(8,128)S(1)} %get-tuple-element.15), channel_id=1, source_target_pairs={{0,96},{32,64},{64,32},{96,0},{128,224},{160,192},{192,160},{224,1... | collective-permute-start | bytes 491528 | tf_op jit(solution)/shard_map/ppermute | solution.py:29
  102.8 10.2 %collective-permute-start.4 = (f32[5,4,8,256]{3,2,1,0:T(8,128)S(1)}, f32[5,4,8,256]{3,2,1,0:T(8,128)S(1)}, u32[]{:S(2)}, u32[]{:S(2)}) collective-permute-start(f32[5,4,8,256]{3,2,1,0:T(8,128)S(1)} %get-tuple-element.14), channel_id=1, source_target_pairs={{0,128},{32,160},{64,192},{96,224},{128,0},{160,32},{192,64},{224,... | collective-permute-start | bytes 491528 | tf_op jit(solution)/shard_map/ppermute | solution.py:29
  103.2 14.4 %collective-permute-start.5 = (f32[5,4,8,256]{3,2,1,0:T(8,128)S(1)}, f32[5,4,8,256]{3,2,1,0:T(8,128)S(1)}, u32[]{:S(2)}, u32[]{:S(2)}) collective-permute-start(f32[5,4,8,256]{3,2,1,0:T(8,128)S(1)} %get-tuple-element.13), channel_id=1, source_target_pairs={{0,160},{32,128},{64,224},{96,192},{128,32},{160,0},{192,96},{224,... | collective-permute-start | bytes 491528 | tf_op jit(solution)/shard_map/ppermute | solution.py:29
  105.5 13.9 %collective-permute-start.6 = (f32[5,4,8,256]{3,2,1,0:T(8,128)S(1)}, f32[5,4,8,256]{3,2,1,0:T(8,128)S(1)}, u32[]{:S(2)}, u32[]{:S(2)}) collective-permute-start(f32[5,4,8,256]{3,2,1,0:T(8,128)S(1)} %get-tuple-element.12), channel_id=1, source_target_pairs={{0,192},{32,224},{64,128},{96,160},{128,64},{160,96},{192,0},{224,... | collective-permute-start | bytes 491528 | tf_op jit(solution)/shard_map/ppermute | solution.py:29
  106.5 16.8 %collective-permute-start.7 = (f32[5,4,8,256]{3,2,1,0:T(8,128)S(1)}, f32[5,4,8,256]{3,2,1,0:T(8,128)S(1)}, u32[]{:S(2)}, u32[]{:S(2)}) collective-permute-start(f32[5,4,8,256]{3,2,1,0:T(8,128)S(1)} %get-tuple-element.11), channel_id=1, source_target_pairs={{0,224},{32,192},{64,160},{96,128},{128,96},{160,64},{192,32},{224... | collective-permute-start | bytes 491528 | tf_op jit(solution)/shard_map/ppermute | solution.py:29
